TPU v7x, 32 devices: a whole 2x2x4 slice. The times are simulated.
32 devices in a mesh: fsdp: 8 (over z, x), rep: 4 (over y, core).
Axes of the slice: x: 2, y: 2, z: 4, core: 2. Of those that a mesh axis runs over, the one named last changes fastest.
Arguments:
- layer_input: bfloat16 [32768, 768], P(('fsdp', 'rep')), may hold values from -6 to 6
- qkv_weight: bfloat16 [768, 2304], P('fsdp'), may hold values from -0.21875 to 0.21875
- attn_weight: bfloat16 [768, 768], P('fsdp'), may hold values from -1.75 to 1.75
- wide_weight: bfloat16 [768, 2304], P('fsdp'), may hold values from -0.21875 to 0.21875
- narrow_weight: bfloat16 [768, 1152], P('fsdp'), may hold values from -0.375 to 0.375
- first_gain: bfloat16 [768], P('fsdp'), may hold values from 0.099609375 to 1.8984375
- second_gain: bfloat16 [768], P('fsdp'), may hold values from 0.099609375 to 1.8984375
- out_grad: bfloat16 [32768, 768], P(('fsdp', 'rep')), may hold values from -12 to 12
- token_seg: int32 [32768], P(('fsdp', 'rep')), may hold values from 0 to 255, as said below
- token_live: int32 [32768], P(('fsdp', 'rep')), may hold values from 0 to 1, as said below
Outputs:
- layer_output: bfloat16 [32768, 768], P(('fsdp', 'rep'))
- input_grad: float32 [32768, 768], P(('fsdp', 'rep'))
- qkv_grad: float32 [768, 2304], P('fsdp')
- attn_grad: float32 [768, 768], P('fsdp')
- wide_grad: float32 [768, 2304], P('fsdp')
- narrow_grad: float32 [768, 1152], P('fsdp')
- first_grad: float32 [768], P('fsdp')
- second_grad: float32 [768], P('fsdp')
Inputs may be any that keep to these rules, and one draw needn't show every extreme that they name: `token_seg`: numbers never fall along the slots; all slots of one number lie in one block of 1024 slots (one device's), and each number begins at a multiple of 128; every block begins a new number; the last tile of the last block begins a number of its own. `token_live`: within each number of token_seg the live slots come first and its first slot is live; in every draw one block of 1024 slots holds a single number with every slot live.
All inputs are finite; a program needn't handle non-finite values.
Results may differ from a plain program's by a relative error of at most 0.018.
Values may be sent and summed in bfloat16 or wider, within the bound.
A program may use at most 320 MiB of HBM per device.

v0:
```python
import functools
import math

import jax
import jax.numpy as jnp
import numpy as np
from jax import lax
from jax.experimental import pallas as pl
from jax.experimental.pallas import tpu as pltpu
from jax.sharding import PartitionSpec as P

HDIM = 64
TILE = 128
PAIR = 128
QROWS = 256


rope_base = 160000.0
eps = 1e-05
masked_score = -1e30


def layer_norm(values, scales):
    center = values - jnp.mean(values, axis=-1, keepdims=True)
    spread = jnp.mean(center * center, axis=-1, keepdims=True)
    return center * lax.rsqrt(spread + eps) * scales


def rope_tables(seg_rows):
    length = seg_rows.shape[0]
    firsts = seg_rows[::TILE]
    before = jnp.sum((firsts[None, :] < seg_rows[:, None]).astype(jnp.int32), axis=1)
    places = jnp.arange(length, dtype=jnp.int32) - TILE * before
    freq_index = jnp.arange(HDIM // 2, dtype=jnp.float32)
    inverse = jnp.exp(freq_index * (-2.0 * math.log(rope_base) / HDIM))
    angles = places.astype(jnp.float32)[:, None] * inverse[None, :]
    cosine, sine = jnp.cos(angles), jnp.sin(angles)
    cos_tab = jnp.concatenate([cosine] * 4, axis=1)
    sin_tab = jnp.concatenate([-sine, sine, -sine, sine], axis=1)
    return cos_tab, sin_tab


def mask_columns(seg_rows, live_rows):
    length = seg_rows.shape[0]
    firsts = seg_rows[::TILE]
    same = seg_rows[:, None] == firsts[None, :]
    query_cols = jnp.where(same, 0.0, masked_score)
    key_cols = jnp.where(same, 1.0, 0.0)
    query_cols = jnp.concatenate([query_cols, jnp.ones((length, 1))], axis=1)
    dead = jnp.where(live_rows > 0, 0.0, masked_score)[:, None]
    key_cols = jnp.concatenate([key_cols, dead], axis=1)
    spare = ((0, 0), (0, HDIM - query_cols.shape[1]))
    return (
        jnp.pad(query_cols, spare).astype(jnp.bfloat16),
        jnp.pad(key_cols, spare).astype(jnp.bfloat16),
    )


def swap_halves(values):
    lane = lax.broadcasted_iota(jnp.int32, values.shape, 1)
    return jnp.where(
        lane % HDIM < HDIM // 2,
        pltpu.roll(values, PAIR - HDIM // 2, 1),
        pltpu.roll(values, HDIM // 2, 1),
    )


def rows_dot(left, right):
    return lax.dot_general(left, right, (((1,), (1,)), ((), ())), preferred_element_type=jnp.float32)


def attend_kernel(pq, pk, pv, cos_ref, sin_ref, qm, km, q_out, k_out, v_out, mixed_out, lse_out):
    cos_tab, sin_tab = cos_ref[...], sin_ref[...]
    length = cos_tab.shape[0]
    q_out[...] = ((pq[...] * cos_tab + swap_halves(pq[...]) * sin_tab).astype(jnp.bfloat16)) * 0.125
    k_out[...] = (pk[...] * cos_tab + swap_halves(pk[...]) * sin_tab).astype(jnp.bfloat16)
    v_out[...] = pv[...].astype(jnp.bfloat16)
    flipped = jnp.transpose(v_out[...])
    for begin in range(0, length, QROWS):
        parts = []
        for head in range(PAIR // HDIM):
            cols = slice(head * HDIM, (head + 1) * HDIM)
            keys = jnp.concatenate([k_out[:, cols], km[...]], axis=1)
            rows = jnp.concatenate(
                [q_out[begin : begin + QROWS, cols], qm[begin : begin + QROWS, :]], axis=1
            )
            scores = rows_dot(keys, rows)
            top = jnp.max(scores, axis=0, keepdims=True)
            expo = jnp.exp(scores - top)
            total = jnp.sum(expo, axis=0, keepdims=True)
            lse_out[0, head : head + 1, begin : begin + QROWS] = top + jnp.log(total)
            out = jnp.dot(
                flipped[cols, :], expo.astype(jnp.bfloat16), preferred_element_type=jnp.float32
            )
            parts.append(out / total)
        both = jnp.concatenate(parts, axis=0)
        mixed_out[begin : begin + QROWS, :] = jnp.transpose(both).astype(jnp.bfloat16)


def attend_back_kernel(
    q_ref, k_ref, v_ref, mixed_ref, go_ref, lse_ref, cos_ref, sin_ref, qm, km, gq_out, gk_out, gv_out
):
    cos_tab, sin_tab = cos_ref[...], sin_ref[...]
    length = cos_tab.shape[0]
    product = jnp.transpose(mixed_ref[...].astype(jnp.float32) * go_ref[...].astype(jnp.float32))
    flipped = jnp.transpose(k_ref[...])
    gq_parts, gk_parts, gv_parts = [], [], []
    for head in range(PAIR // HDIM):
        cols = slice(head * HDIM, (head + 1) * HDIM)
        delta = jnp.sum(product[cols, :], axis=0, keepdims=True)
        keys = jnp.concatenate([k_ref[:, cols], km[...]], axis=1)
        values = v_ref[:, cols]
        grad_k = jnp.zeros((length, HDIM), jnp.float32)
        grad_v = jnp.zeros((length, HDIM), jnp.float32)
        grad_q = []
        for begin in range(0, length, QROWS):
            span = slice(begin, begin + QROWS)
            low_q, low_go = q_ref[span, cols], go_ref[span, cols]
            scores = rows_dot(keys, jnp.concatenate([low_q, qm[span, :]], axis=1))
            probs = jnp.exp(scores - lse_ref[0, head : head + 1, span])
            grad_v += jnp.dot(probs.astype(jnp.bfloat16), low_go, preferred_element_type=jnp.float32)
            grad_p = rows_dot(values, low_go)
            grad_s = (probs * (grad_p - delta[:, span])).astype(jnp.bfloat16)
            grad_k += jnp.dot(grad_s, low_q, preferred_element_type=jnp.float32)
            grad_q.append(jnp.dot(flipped[cols, :], grad_s, preferred_element_type=jnp.float32))
        gq_parts.append(jnp.concatenate(grad_q, axis=1))
        gk_parts.append(grad_k)
        gv_parts.append(grad_v)
    grad_q = jnp.transpose(jnp.concatenate(gq_parts, axis=0)) * 0.125
    grad_k = jnp.concatenate(gk_parts, axis=1)
    gq_out[...] = (grad_q * cos_tab + swap_halves(grad_q * sin_tab)).astype(jnp.bfloat16)
    gk_out[...] = (grad_k * cos_tab + swap_halves(grad_k * sin_tab)).astype(jnp.bfloat16)
    gv_out[...] = jnp.concatenate(gv_parts, axis=1).astype(jnp.bfloat16)


def attend(packed, cos_tab, sin_tab, qm, km):
    length, width = packed.shape[0], packed.shape[1] // 3
    pairs = width // PAIR
    block = lambda shift: pl.BlockSpec((length, PAIR), lambda i: (0, i + shift))
    table = pl.BlockSpec((length, PAIR), lambda i: (0, 0))
    mask = pl.BlockSpec((length, HDIM), lambda i: (0, 0))
    rows = jax.ShapeDtypeStruct((length, width), jnp.bfloat16)
    return pl.pallas_call(
        attend_kernel,
        grid=(pairs,),
        in_specs=[block(0), block(pairs), block(2 * pairs), table, table, mask, mask],
        out_specs=[block(0)] * 4 + [pl.BlockSpec((1, 2, length), lambda i: (i, 0, 0))],
        out_shape=[rows] * 4 + [jax.ShapeDtypeStruct((pairs, 2, length), jnp.float32)],
        compiler_params=pltpu.CompilerParams(vmem_limit_bytes=40 << 20),
        cost_estimate=pl.CostEstimate(
            flops=16 * width * length * length, bytes_accessed=20 * length * width,
            transcendentals=pairs * 2 * length * length,
        ),
    )(packed, packed, packed, cos_tab, sin_tab, qm, km)


def attend_back(queries, keyset, valueset, mixed, grad_mixed, lse, cos_tab, sin_tab, qm, km):
    length, width = queries.shape
    pairs = width // PAIR
    block = pl.BlockSpec((length, PAIR), lambda i: (0, i))
    table = pl.BlockSpec((length, PAIR), lambda i: (0, 0))
    mask = pl.BlockSpec((length, HDIM), lambda i: (0, 0))
    rows = jax.ShapeDtypeStruct((length, width), jnp.bfloat16)
    return pl.pallas_call(
        attend_back_kernel,
        grid=(pairs,),
        in_specs=[block] * 5
        + [pl.BlockSpec((1, 2, length), lambda i: (i, 0, 0)), table, table, mask, mask],
        out_specs=[block] * 3,
        out_shape=[rows] * 3,
        compiler_params=pltpu.CompilerParams(vmem_limit_bytes=48 << 20),
        cost_estimate=pl.CostEstimate(
            flops=40 * width * length * length, bytes_accessed=16 * length * width,
            transcendentals=pairs * 2 * length * length,
        ),
    )(queries, keyset, valueset, mixed, grad_mixed, lse, cos_tab, sin_tab, qm, km)


def swap_with(array, axis, bit):
    size = lax.axis_size(axis)
    return lax.ppermute(array, axis, [(i, i ^ (1 << bit)) for i in range(size)])


def side_of(axis, bit):
    return (lax.axis_index(axis) >> bit) & 1


def bits_of(axis):
    return [(axis, bit) for bit in reversed(range(lax.axis_size(axis).bit_length() - 1))]


def gather_half(piece, order):
    canon = bits_of("fsdp") + bits_of("rep")
    have = []
    for axis, bit in order:
        other = swap_with(piece, axis, bit)
        side = side_of(axis, bit) == 0
        place = sum(canon.index(known) < canon.index((axis, bit)) for known in have)
        piece = jnp.stack(
            [jnp.where(side, piece, other), jnp.where(side, other, piece)], axis=place
        )
        have.append((axis, bit))
    return piece.reshape(-1, piece.shape[-1])


def pick(array, dim, side):
    return lax.dynamic_index_in_dim(array, side, dim, keepdims=False)


def orders():
    rep_bits, fsdp_bits = bits_of("rep")[::-1], bits_of("fsdp")[::-1]
    near, far = rep_bits[0], rep_bits[1:]
    one = [near] + far + fsdp_bits
    two = [near] + fsdp_bits[:1] + far + fsdp_bits[1:]
    return one, two


def gather_weights(arrays):
    joint = jnp.concatenate(arrays, axis=1)
    for axis, bit in bits_of("rep"):
        size = joint.shape[0] // 2
        joint = lax.dynamic_slice_in_dim(joint, side_of(axis, bit) * size, size, axis=0)
    cut = joint.shape[1] // 256 * 128
    one, two = orders()
    whole = jnp.concatenate(
        [gather_half(joint[:, :cut], one[::-1]), gather_half(joint[:, cut:], two[::-1])], axis=1
    )
    outs, start = [], 0
    for array in arrays:
        outs.append(whole[:, start : start + array.shape[1]])
        start += array.shape[1]
    return outs


def scatter_half(term, order):
    canon = bits_of("fsdp") + bits_of("rep")
    rows = term.shape[0] >> len(canon)
    acc = term.reshape([2] * len(canon) + [rows, term.shape[1]])
    left = list(canon)
    for axis, bit in order:
        dim = left.index((axis, bit))
        side = side_of(axis, bit)
        other = swap_with(pick(acc, dim, 1 - side), axis, bit)
        acc = pick(acc, dim, side).astype(jnp.float32) + other.astype(jnp.float32)
        acc = acc.astype(jnp.bfloat16)
        left.remove((axis, bit))
    rep_order = [entry for entry in order[::-1] if entry[0] == "rep"]
    have = []
    for axis, bit in rep_order:
        other = swap_with(acc, axis, bit)
        side = side_of(axis, bit) == 0
        place = sum(canon.index(known) < canon.index((axis, bit)) for known in have)
        acc = jnp.stack([jnp.where(side, acc, other), jnp.where(side, other, acc)], axis=place)
        have.append((axis, bit))
    return acc.reshape(-1, acc.shape[-1]).astype(jnp.float32)


def scatter_sums(terms):
    joint = jnp.concatenate([term.astype(jnp.bfloat16) for term in terms], axis=1)
    cut = joint.shape[1] // 256 * 128
    one, two = orders()
    whole = jnp.concatenate(
        [scatter_half(joint[:, :cut], one), scatter_half(joint[:, cut:], two)], axis=1
    )
    outs, start = [], 0
    for term in terms:
        outs.append(whole[:, start : start + term.shape[1]])
        start += term.shape[1]
    return outs


def geglu(lifted):
    half_ff = lifted.shape[1] // 2
    return jax.nn.gelu(lifted[:, :half_ff], approximate=False) * lifted[:, half_ff:]


MESH = pl.DeviceIdType.MESH
HALF = 48
AHEAD = 4
GATHER_LAGS = (3.0 - 2.1 * AHEAD, 3.0, 7.5, 12.0, 15.0)
PACE = 2.1
PAIR_US = 6.0
STEP = 16


def table_constants(length):
    places = np.arange(length, dtype=np.float32)
    freq_index = np.arange(HDIM // 2, dtype=np.float32)
    inverse = np.exp(freq_index * np.float32(-2.0 * math.log(rope_base) / HDIM)).astype(np.float32)
    angles = (places[:, None] * inverse[None, :]).astype(np.float32).astype(np.float64)
    cosine, sine = np.cos(angles), np.sin(angles)
    cos_tab = np.concatenate([cosine] * 4, axis=1).astype(np.float32)
    sin_tab = np.concatenate([-sine, sine, -sine, sine], axis=1).astype(np.float32)
    return cos_tab, sin_tab


class Place:
    def __init__(self):
        self.f = lax.axis_index("fsdp")
        self.r = lax.axis_index("rep")
        self.z = self.f // 2
        self.x = self.f % 2
        self.y = self.r // 2
        self.core = self.r % 2

    def flip(self, value, bit):
        size = 1 << bit
        return value + size - 2 * size * ((value // size) % 2)

    def along_z(self, d):
        z = self.z
        for bit in range(2):
            if (d >> bit) & 1:
                z = self.flip(z, bit)
        return z

    def fsdp_of(self, m):
        f = self.f
        for bit in range(3):
            if (m >> bit) & 1:
                f = self.flip(f, bit)
        return f

    def z_dev(self, d):
        return (2 * self.along_z(d) + self.x, self.r)

    def x_dev(self):
        return (self.flip(self.f, 0), self.r)

    def y_dev(self):
        return (self.f, self.flip(self.r, 1))

    def core_dev(self):
        return (self.f, self.flip(self.r, 0))

    def rows_zx(self):
        return pl.ds(pl.multiple_of(HALF * self.core + STEP * self.y, STEP), 2 * STEP)

    def rows_y(self):
        return pl.ds(pl.multiple_of(HALF * self.core + 2 * STEP * self.y, STEP), STEP)

    def rows_core(self):
        return pl.ds(pl.multiple_of(HALF * self.core, STEP), HALF)


def remote(src, dst, send, recv, dev):
    return pltpu.make_async_remote_copy(
        src_ref=src, dst_ref=dst, send_sem=send, recv_sem=recv, device_id=dev, device_id_type=MESH
    )


def staged(count, lags, pace):
    return sorted((lag + pace * k, stage, k) for stage, lag in enumerate(lags) for k in range(count))


class Gather:
    def __init__(self, place, sources, targets, send, recv, own):
        self.p, self.src, self.dst = place, sources, targets
        self.send, self.recv, self.own = send, recv, own
        self.count = len(sources)

    def z_copy(self, k, d):
        p, rows = self.p, self.p.rows_zx()
        return remote(
            self.src[k].at[rows, :],
            self.dst[k].at[p.z, p.x, rows, :],
            self.send.at[k, d - 1],
            self.recv.at[k, d - 1],
            p.z_dev(d),
        )

    def own_copy(self, k):
        p, rows = self.p, self.p.rows_zx()
        return pltpu.make_async_copy(
            self.src[k].at[rows, :], self.dst[k].at[p.z, p.x, rows, :], self.own.at[k]
        )

    def x_copy(self, k):
        p = self.p
        part = self.dst[k].at[:, p.x, p.rows_zx(), :]
        return remote(part, part, self.send.at[k, 3], self.recv.at[k, 3], p.x_dev())

    def y_copy(self, k):
        p = self.p
        part = self.dst[k].at[:, :, p.rows_y(), :]
        return remote(part, part, self.send.at[k, 4], self.recv.at[k, 4], p.y_dev())

    def core_copy(self, k):
        p = self.p
        part = self.dst[k].at[:, :, p.rows_core(), :]
        return remote(part, part, self.send.at[k, 5], self.recv.at[k, 5], p.core_dev())

    def step(self, stage, k):
        if stage == 0:
            self.own_copy(k).start()
            for d in (1, 2, 3):
                self.z_copy(k, d).start()
        elif stage == 1:
            self.own_copy(k).wait()
            for d in (1, 2, 3):
                self.z_copy(k, d).wait_recv()
            self.x_copy(k).start()
        elif stage == 2:
            self.x_copy(k).wait_recv()
            self.y_copy(k).start()
        elif stage == 3:
            self.y_copy(k).wait_recv()
            self.core_copy(k).start()
        else:
            self.core_copy(k).wait_recv()

    def finish(self):
        for k in range(self.count):
            for d in (1, 2, 3):
                self.z_copy(k, d).wait_send()
            self.x_copy(k).wait_send()
            self.y_copy(k).wait_send()
            self.core_copy(k).wait_send()


def greet(devices):
    barrier = pltpu.get_barrier_semaphore()
    for dev in devices:
        pl.semaphore_signal(barrier, inc=1, device_id=dev, device_id_type=MESH)
    pl.semaphore_wait(barrier, len(devices))


def forward_kernel(
    plan,
    seg_ref,
    x_ref,
    gain_in,
    live_ref,
    cos_in,
    sin_in,
    wq_in,
    wa_in,
    ww_in,
    wn_in,
    q_out,
    k_out,
    v_out,
    mixed_out,
    lse_out,
    normed_out,
    gain_out,
    wq_all,
    wa_all,
    ww_all,
    wn_all,
    cos_tab,
    sin_tab,
    qm,
    km,
    gain_send,
    gain_recv,
    wbuf,
    send,
    recv,
    own,
    gain_send_sem,
    gain_recv_sem,
    load_sem,
    score_buf,
):
    i = pl.program_id(0)
    pairs = pl.num_programs(0)
    npairs, cuts = plan
    place = Place()
    length, width = x_ref.shape
    tiles = length // TILE
    sources = [wq_in.at[k] for k in range(npairs)]
    targets = [wq_all.at[k] for k in range(npairs)]
    for cut, shard, full in zip(cuts, (wa_in, ww_in, wn_in), (wa_all, ww_all, wn_all)):
        for lo, size in cut:
            sources.append(shard.at[:, pl.ds(lo, size)])
            targets.append(full.at[:, :, :, pl.ds(lo, size)])
    gather = Gather(place, sources, targets, send, recv, own)

    events = staged(gather.count, GATHER_LAGS, PACE)
    events = [e for e in events if e[1:] not in [(0, k) for k in range(AHEAD)]]

    def run_until(time):
        while events and events[0][0] <= time:
            gather.step(*events.pop(0)[1:])

    def gain_copy(m):
        return remote(
            gain_send,
            gain_recv.at[place.f],
            gain_send_sem.at[m - 1],
            gain_recv_sem.at[m - 1],
            (place.fsdp_of(m), place.r),
        )

    def load(k):
        return pltpu.make_async_copy(wq_all.at[k], wbuf.at[k % 2], load_sem.at[k % 2])

    @pl.when(i == 0)
    def _():
        gain_send[...] = gain_in[...]
        greet(
            [(place.fsdp_of(m), place.r) for m in range(1, 8)] + [place.y_dev(), place.core_dev()]
        )
        for m in range(1, 8):
            gain_copy(m).start()
        for k in range(AHEAD):
            gather.step(0, k)
        gain_recv[place.f] = gain_in[...]
        lane_tile = lax.broadcasted_iota(jnp.int32, (TILE, HDIM), 1)
        live_cols = jnp.transpose(
            jnp.concatenate(
                [live_ref[...].astype(jnp.float32), jnp.zeros((TILE - tiles, TILE), jnp.float32)], axis=0
            )
        )
        segs = [seg_ref[u : u + 1, :] for u in range(tiles)]
        for t in range(tiles):
            rows = slice(t * TILE, (t + 1) * TILE)
            before = jnp.zeros((1, TILE), jnp.int32)
            same = jnp.zeros((TILE, HDIM), jnp.float32)
            for u in range(tiles):
                before += jnp.where(segs[u] < segs[t], 1, 0)
                hit = jnp.where(segs[u] == segs[t], 1.0, 0.0)[:, :HDIM]
                same = jnp.where(lane_tile == u, hit, same)
            cos_t, sin_t = cos_in[:TILE, :], sin_in[:TILE, :]
            for c in range(1, t + 1):
                at = slice(c * TILE, (c + 1) * TILE)
                cos_t = jnp.where(t - before == c, cos_in[at, :], cos_t)
                sin_t = jnp.where(t - before == c, sin_in[at, :], sin_t)
            cos_tab[rows, :] = cos_t
            sin_tab[rows, :] = sin_t
            dead = jnp.where(live_cols[:, t : t + 1] > 0, 0.0, masked_score)
            qv = jnp.where(lane_tile < tiles, jnp.where(same > 0, 0.0, masked_score), 0.0)
            qm[rows, :] = jnp.where(lane_tile == tiles, 1.0, qv).astype(jnp.bfloat16)
            kv = jnp.where(lane_tile == tiles, dead, same)
            km[rows, :] = kv.astype(jnp.bfloat16)
        run_until(3.0)
        for m in range(1, 8):
            gain_copy(m).wait()
        part = width // 8
        wide_row = lax.broadcasted_iota(jnp.int32, (PAIR, width), 0)
        wide_col = lax.broadcasted_iota(jnp.int32, (PAIR, width), 1)
        gains = jnp.zeros((8, width), jnp.float32)
        for f in range(8):
            pick_f = jnp.where((wide_col == wide_row + f * part) & (wide_row < part), 1.0, 0.0)
            gains += jnp.dot(
                gain_recv[f].astype(jnp.bfloat16),
                pick_f.astype(jnp.bfloat16),
                preferred_element_type=jnp.float32,
            )
        gain_out[...] = gains
        run_until(6.4)

        def norm_rows(b, carry):
            rows = pl.ds(pl.multiple_of(b * TILE, TILE), TILE)
            v = x_ref[rows, :].astype(jnp.float32)
            c = v - jnp.mean(v, axis=1, keepdims=True)
            spread = jnp.mean(c * c, axis=1, keepdims=True)
            normed_out[rows, :] = (c * lax.rsqrt(spread + eps) * gain_out[0:1, :]).astype(jnp.bfloat16)
            return carry

        lax.fori_loop(0, tiles, norm_rows, 0)
        run_until(GATHER_LAGS[4])
        load(0).start()
        load(0).wait()

    packed = jnp.dot(
        normed_out[...],
        wbuf[i % 2].reshape(width, 3 * PAIR),
        preferred_element_type=jnp.float32,
    )
    pq, pk, pv = packed[:, :PAIR], packed[:, PAIR : 2 * PAIR], packed[:, 2 * PAIR :]
    cos_v, sin_v = cos_tab[...], sin_tab[...]
    q_out[...] = ((pq * cos_v + swap_halves(pq) * sin_v).astype(jnp.bfloat16)) * 0.125
    k_out[...] = (pk * cos_v + swap_halves(pk) * sin_v).astype(jnp.bfloat16)
    v_out[...] = pv.astype(jnp.bfloat16)
    flipped = jnp.transpose(v_out[...])

    slots = 4
    queue = [[[] for _ in range(slots)] for _ in range(npairs)]
    for p in range(npairs):
        for slot in range(slots):
            now = GATHER_LAGS[4] + PAIR_US * (p + (slot + 1) / slots)
            while events and events[0][0] <= now:
                queue[p][slot].append(events.pop(0)[1:])
    queue[-1][-1].extend(e[1:] for e in events)

    def run_slot(slot):
        for p in range(npairs):

            @pl.when(i == p)
            def _():
                for stage, k in queue[p][slot]:
                    gather.step(stage, k)
                if p + 1 < npairs and slot == slots - 2:
                    load(p + 1).start()
                if p + 1 < npairs and slot == slots - 1:
                    load(p + 1).wait()

    parts = []
    for head in range(PAIR // HDIM):
        run_slot(2 * head)
        cols = slice(head * HDIM, (head + 1) * HDIM)
        keys = jnp.concatenate([k_out[:, cols], km[...]], axis=1)
        rows = jnp.concatenate([q_out[:, cols], qm[...]], axis=1)
        tops = []
        for begin in range(0, length, QROWS):
            scores = rows_dot(keys[begin : begin + QROWS, :], rows)
            score_buf[head, begin : begin + QROWS, :] = scores
            tops.append(jnp.max(scores.reshape(QROWS // 8, 8, length), axis=0))
        top = jnp.max(functools.reduce(jnp.maximum, tops), axis=0, keepdims=True)
        run_slot(2 * head + 1)
        out = jnp.zeros((HDIM, length), jnp.float32)
        sums = jnp.zeros((8, length), jnp.float32)
        for begin in range(0, length, QROWS):
            expo = jnp.exp(score_buf[head, begin : begin + QROWS, :] - top)
            sums += jnp.sum(expo.reshape(QROWS // 8, 8, length), axis=0)
            out += jnp.dot(
                flipped[cols, begin : begin + QROWS],
                expo.astype(jnp.bfloat16),
                preferred_element_type=jnp.float32,
            )
        total = jnp.sum(sums, axis=0, keepdims=True)
        lse_out[0, head : head + 1, :] = top + jnp.log(total)
        parts.append(out / total)
    mixed_out[...] = jnp.transpose(jnp.concatenate(parts, axis=0)).astype(jnp.bfloat16)

    @pl.when(i == pairs - 1)
    def _():
        gather.finish()


def cuts_of(width, piece):
    return [(lo, min(piece, width - lo)) for lo in range(0, width, piece)]


def forward(layer_input, wq_in, attn_weight, wide_weight, narrow_weight, gain_in, token_seg, token_live):
    length, width = layer_input.shape
    pairs = width // PAIR
    part = attn_weight.shape[0]
    cos_c, sin_c = table_constants(length)
    cuts = [cuts_of(w.shape[1], 3 * PAIR) for w in (attn_weight, wide_weight, narrow_weight)]
    count = pairs + sum(len(c) for c in cuts)
    block = pl.BlockSpec((length, PAIR), lambda i: (0, i))
    whole = pl.BlockSpec(memory_space=pltpu.VMEM)
    hbm = pl.BlockSpec(memory_space=pl.ANY)
    rows = jax.ShapeDtypeStruct((length, width), jnp.bfloat16)
    full = lambda cols: jax.ShapeDtypeStruct((4, 2, part, cols), jnp.bfloat16)
    return pl.pallas_call(
        functools.partial(forward_kernel, (pairs, cuts)),
        grid=(pairs,),
        in_specs=[whole] * 6 + [hbm] * 4,
        out_specs=[block] * 4
        + [pl.BlockSpec((1, 2, length), lambda i: (i, 0, 0)), whole, whole]
        + [hbm] * 4
        + [whole] * 4,
        out_shape=[rows] * 4
        + [
            jax.ShapeDtypeStruct((pairs, 2, length), jnp.float32),
            rows,
            jax.ShapeDtypeStruct((8, width), jnp.float32),
            jax.ShapeDtypeStruct((pairs, 4, 2, part, 3 * PAIR), jnp.bfloat16),
            full(width),
            full(wide_weight.shape[1]),
            full(narrow_weight.shape[1]),
            jax.ShapeDtypeStruct((length, PAIR), jnp.float32),
            jax.ShapeDtypeStruct((length, PAIR), jnp.float32),
            jax.ShapeDtypeStruct((length, HDIM), jnp.bfloat16),
            jax.ShapeDtypeStruct((length, HDIM), jnp.bfloat16),
        ],
        scratch_shapes=[
            pltpu.VMEM((8, PAIR), jnp.float32),
            pltpu.VMEM((8, 8, PAIR), jnp.float32),
            pltpu.VMEM((2, 4, 2, part, 3 * PAIR), jnp.bfloat16),
            pltpu.SemaphoreType.DMA((count, 6)),
            pltpu.SemaphoreType.DMA((count, 6)),
            pltpu.SemaphoreType.DMA((count,)),
            pltpu.SemaphoreType.DMA((7,)),
            pltpu.SemaphoreType.DMA((7,)),
            pltpu.SemaphoreType.DMA((2,)),
            pltpu.VMEM((2, length, length), jnp.float32),
        ],
        compiler_params=pltpu.CompilerParams(
            vmem_limit_bytes=56 << 20, collective_id=0, has_side_effects=True
        ),
        cost_estimate=pl.CostEstimate(
            flops=22 * width * length * length, bytes_accessed=40 * length * width,
            transcendentals=pairs * 2 * length * length,
        ),
    )(
        token_seg.reshape(length // TILE, TILE), layer_input, gain_in,
        token_live.reshape(length // TILE, TILE),
        jnp.asarray(cos_c), jnp.asarray(sin_c), wq_in, attn_weight, wide_weight, narrow_weight,
    )


class Reduce:
    def __init__(self, place, sources, loaded, outs, bufs, send, recv, load):
        self.p, self.src, self.loaded, self.outs = place, sources, loaded, outs
        self.acc, self.rc, self.ry, self.rx, self.rz, self.s, self.ry2, self.f, self.rf = bufs
        self.send, self.recv, self.load = send, recv, load
        self.count = len(sources)

    def local(self, start, size):
        return pl.ds(pl.multiple_of(start, STEP), size)

    def mine(self):
        return self.local(STEP * self.p.y, 2 * STEP)

    def core_copy(self, k):
        p = self.p
        rows = self.local(HALF * (1 - p.core), HALF)
        return remote(
            self.src[k].at[:, :, rows, :], self.rc.at[k], self.send.at[k, 0], self.recv.at[k, 0], p.core_dev()
        )

    def load_copy(self, k):
        return pltpu.make_async_copy(
            self.src[k].at[:, :, self.p.rows_core(), :], self.acc.at[k], self.load.at[k]
        )

    def y_copy(self, k):
        p = self.p
        rows = self.local(2 * STEP * (1 - p.y), STEP)
        return remote(
            self.acc.at[k, :, :, rows, :], self.ry.at[k], self.send.at[k, 1], self.recv.at[k, 1], p.y_dev()
        )

    def x_copy(self, k):
        p = self.p
        return remote(
            self.acc.at[k, :, 1 - p.x, self.mine(), :],
            self.rx.at[k],
            self.send.at[k, 2],
            self.recv.at[k, 2],
            p.x_dev(),
        )

    def z_copy(self, k, d):
        p = self.p
        return remote(
            self.acc.at[k, p.along_z(d), p.x, self.mine(), :],
            self.rz.at[k, d - 1],
            self.send.at[k, 2 + d],
            self.recv.at[k, 2 + d],
            p.z_dev(d),
        )

    def y2_copy(self, k):
        return remote(
            self.s.at[k], self.ry2.at[k], self.send.at[k, 6], self.recv.at[k, 6], self.p.y_dev()
        )

    def core2_copy(self, k):
        return remote(
            self.f.at[k], self.rf.at[k], self.send.at[k, 7], self.recv.at[k, 7], self.p.core_dev()
        )

    def plus(self, a, b):
        return (a.astype(jnp.float32) + b.astype(jnp.float32)).astype(jnp.bfloat16)

    def step(self, stage, k):
        p = self.p
        acc = self.acc
        if stage == 0:
            self.core_copy(k).start()
            if self.loaded[k]:
                self.load_copy(k).start()
        elif stage == 1:
            self.core_copy(k).wait_recv()
            if self.loaded[k]:
                self.load_copy(k).wait()
                acc[k] = self.plus(acc[k], self.rc[k])
            else:
                acc[k] = self.plus(self.src[k][:, :, p.rows_core(), :], self.rc[k])
            self.y_copy(k).start()
        elif stage == 2:
            self.y_copy(k).wait_recv()
            rows = self.local(2 * STEP * p.y, STEP)
            acc[k, :, :, rows, :] = self.plus(acc[k, :, :, rows, :], self.ry[k])
            self.x_copy(k).start()
        elif stage == 3:
            self.x_copy(k).wait_recv()
            rows = self.mine()
            acc[k, :, p.x, rows, :] = self.plus(acc[k, :, p.x, rows, :], self.rx[k])
            for d in (2, 3, 1):
                self.z_copy(k, d).start()
        elif stage == 4:
            total = acc[k, p.z, p.x, self.mine(), :].astype(jnp.float32)
            for d in (1, 2, 3):
                self.z_copy(k, d).wait_recv()
                total += self.rz[k, d - 1].astype(jnp.float32)
            self.s[k] = total.astype(jnp.bfloat16)
            self.y2_copy(k).start()
        elif stage == 5:
            self.y2_copy(k).wait_recv()
            low, high = self.local(STEP * p.y, STEP), self.local(STEP * (1 - p.y), STEP)
            self.f[k, self.local(2 * STEP * p.y, STEP), :] = self.s[k, low, :]
            self.f[k, STEP : 2 * STEP, :] = self.plus(self.s[k, high, :], self.ry2[k, low, :])
            self.f[k, self.local(2 * STEP * (1 - p.y), STEP), :] = self.ry2[k, high, :]
            self.core2_copy(k).start()
            self.outs[k][p.rows_core(), :] = self.f[k].astype(jnp.float32)
        else:
            self.core2_copy(k).wait_recv()
            self.outs[k][self.local(HALF * (1 - p.core), HALF), :] = self.rf[k].astype(jnp.float32)

    def finish(self):
        for k in range(self.count):
            self.core_copy(k).wait_send()
            self.y_copy(k).wait_send()
            self.x_copy(k).wait_send()
            for d in (1, 2, 3):
                self.z_copy(k, d).wait_send()
            self.y2_copy(k).wait_send()
            self.core2_copy(k).wait_send()


REDUCE_LAGS = (0.0, 4.0, 10.0, 16.0, 22.0, 28.0, 32.0)
BACK_US = 8.6


def reduce_events(given, pairs):
    now, first, late, starts = 0.0, 0, 0, {}
    while first < given or late < pairs:
        if late < pairs and BACK_US * (late + 1) <= now:
            starts[given + late] = BACK_US * (late + 1)
            late += 1
        elif first < given:
            starts[first] = now
            first += 1
        else:
            now = BACK_US * (late + 1)
            continue
        now += 2.35
    return sorted((t + lag, stage, k) for k, t in starts.items() for stage, lag in enumerate(REDUCE_LAGS))


def backward_kernel(
    plan,
    q_ref,
    k_ref,
    v_ref,
    mixed_ref,
    go_ref,
    lse_ref,
    cos_ref,
    sin_ref,
    qm,
    km,
    gain_ref,
    second_ref,
    normed_in,
    x_in,
    gm_in,
    wq_in,
    narrow_in,
    wide_in,
    attn_in,
    input_grad,
    qkv_out,
    attn_out,
    wide_out,
    narrow_out,
    gain_out,
    normed_t,
    x_buf,
    gm_buf,
    wq_buf,
    gp_all,
    terms,
    acc,
    rc,
    ry,
    rx,
    rz,
    s_buf,
    ry2,
    f_buf,
    rf,
    gain_rep,
    gain_parts,
    gain_all,
    send,
    recv,
    load,
    bulk,
    rep_send,
    rep_recv,
    fsdp_send,
    fsdp_recv,
    out_sem,
):
    i = pl.program_id(0)
    npairs, cuts = plan
    place = Place()
    length, width = normed_in.shape
    part = width // 8
    sources, loaded, outs = [], [], []
    for cut, term, out in zip(cuts, (narrow_in, wide_in, attn_in), (narrow_out, wide_out, attn_out)):
        for lo, size in cut:
            sources.append(term.at[:, :, :, pl.ds(lo, size)])
            outs.append(out.at[:, pl.ds(lo, size)])
            loaded.append(True)
    given = len(sources)
    for p in range(npairs):
        sources.append(terms.at[p])
        outs.append(qkv_out.at[p])
        loaded.append(False)
    bufs = (acc, rc, ry, rx, rz, s_buf, ry2, f_buf, rf)
    reduce = Reduce(place, sources, loaded, outs, bufs, send, recv, load)
    events = reduce_events(given, npairs)
    slots = 2 * (length // QROWS)
    queue = [[[] for _ in range(slots + 1)] for _ in range(npairs)]
    for p in range(npairs):
        for slot in range(slots + 1):
            now = BACK_US * (p + min(slot, slots - 0.01) / slots) if slot < slots else BACK_US * (p + 1)
            while events and events[0][0] <= now:
                queue[p][slot].append(events.pop(0)[1:])

    def run_slot(slot):
        for p in range(npairs):
            if queue[p][slot]:

                @pl.when(i == p)
                def _():
                    for stage, k in queue[p][slot]:
                        reduce.step(stage, k)

    bulk_copies = [
        pltpu.make_async_copy(x_in, x_buf, bulk.at[0]),
        pltpu.make_async_copy(gm_in, gm_buf, bulk.at[1]),
        pltpu.make_async_copy(wq_in, wq_buf, bulk.at[2]),
    ]

    @pl.when(i == 0)
    def _():
        greet(
            [(place.fsdp_of(m), place.r) for m in range(1, 8)]
            + [place.y_dev(), place.core_dev(), (place.f, 3 - place.r)]
        )
        for copy in bulk_copies:
            copy.start()
        normed_t[...] = jnp.transpose(normed_in[...])

    cos_tab, sin_tab = cos_ref[...], sin_ref[...]
    product = jnp.transpose(mixed_ref[...].astype(jnp.float32) * go_ref[...].astype(jnp.float32))
    flipped = jnp.transpose(k_ref[...])
    gq_parts, gk_parts, gv_parts = [], [], []
    slot = 0
    for head in range(PAIR // HDIM):
        cols = slice(head * HDIM, (head + 1) * HDIM)
        delta = jnp.sum(product[cols, :], axis=0, keepdims=True)
        keys = jnp.concatenate([k_ref[:, cols], km[...]], axis=1)
        values = v_ref[:, cols]
        grad_k = jnp.zeros((length, HDIM), jnp.float32)
        grad_v = jnp.zeros((length, HDIM), jnp.float32)
        grad_q = []
        for begin in range(0, length, QROWS):
            run_slot(slot)
            slot += 1
            span = slice(begin, begin + QROWS)
            low_q, low_go = q_ref[span, cols], go_ref[span, cols]
            scores = rows_dot(keys, jnp.concatenate([low_q, qm[span, :]], axis=1))
            probs = jnp.exp(scores - lse_ref[0, head : head + 1, span])
            grad_v += jnp.dot(probs.astype(jnp.bfloat16), low_go, preferred_element_type=jnp.float32)
            grad_p = rows_dot(values, low_go)
            grad_s = (probs * (grad_p - delta[:, span])).astype(jnp.bfloat16)
            grad_k += jnp.dot(grad_s, low_q, preferred_element_type=jnp.float32)
            grad_q.append(jnp.dot(flipped[cols, :], grad_s, preferred_element_type=jnp.float32))
        gq_parts.append(jnp.concatenate(grad_q, axis=1))
        gk_parts.append(grad_k)
        gv_parts.append(grad_v)
    grad_q = jnp.transpose(jnp.concatenate(gq_parts, axis=0)) * 0.125
    grad_k = jnp.concatenate(gk_parts, axis=1)
    gp = jnp.concatenate(
        [
            (grad_q * cos_tab + swap_halves(grad_q * sin_tab)).astype(jnp.bfloat16),
            (grad_k * cos_tab + swap_halves(grad_k * sin_tab)).astype(jnp.bfloat16),
            jnp.concatenate(gv_parts, axis=1).astype(jnp.bfloat16),
        ],
        axis=1,
    )
    gp_all[i] = gp
    term = jnp.dot(normed_t[...], gp, preferred_element_type=jnp.float32)
    terms[i] = term.astype(jnp.bfloat16).reshape(4, 2, part, 3 * PAIR)
    run_slot(slots)

    def rep_copy(m):
        return remote(
            gain_rep.at[place.r],
            gain_rep.at[place.r],
            rep_send.at[m - 1],
            rep_recv.at[m - 1],
            (place.f, (place.y_dev()[1], place.core_dev()[1], 3 - place.r)[m - 1]),
        )

    def fsdp_copy(m):
        return remote(
            gain_parts.at[place.fsdp_of(m)],
            gain_all.at[place.f],
            fsdp_send.at[m - 1],
            fsdp_recv.at[m - 1],
            (place.fsdp_of(m), place.r),
        )

    @pl.when(i == npairs - 1)
    def _():
        for copy in bulk_copies:
            copy.wait()
        gain = gain_ref[0:1, :]
        blocks = length // QROWS
        share = len(events) // (blocks + 1)
        first = jnp.zeros((1, width), jnp.float32)
        writes = []
        for b in range(blocks):
            rows = slice(b * QROWS, (b + 1) * QROWS)
            e1 = jnp.zeros((QROWS, width), jnp.float32)
            for p in range(npairs):
                e1 += rows_dot(gp_all[p, rows, :], wq_buf[p].reshape(width, 3 * PAIR))
            v = x_buf[rows, :].astype(jnp.float32)
            c = v - jnp.mean(v, axis=1, keepdims=True)
            r1 = lax.rsqrt(jnp.mean(c * c, axis=1, keepdims=True) + eps)
            n1 = c * r1
            first += jnp.sum(e1 * n1, axis=0, keepdims=True)
            f1 = e1 * gain
            drift = f1 - jnp.mean(f1, axis=1, keepdims=True)
            gm_buf[rows, :] += r1 * (drift - n1 * jnp.mean(f1 * n1, axis=1, keepdims=True))
            write = pltpu.make_async_copy(gm_buf.at[rows, :], input_grad.at[rows, :], out_sem.at[b])
            write.start()
            writes.append(write)
            for _ in range(2):
                if events:
                    reduce.step(*events.pop(0)[1:])
        sub = lax.broadcasted_iota(jnp.int32, (8, width), 0)
        gain_rep[place.r] = jnp.where(sub == 0, first, jnp.where(sub == 1, second_ref[...], 0.0))
        for m in (1, 2, 3):
            rep_copy(m).start()
        for m in (1, 2, 3):
            rep_copy(m).wait()
        total = gain_rep[0] + gain_rep[1] + gain_rep[2] + gain_rep[3]
        gain_parts[...] = jnp.zeros_like(gain_parts)
        for f in range(8):
            gain_parts[f, :, :part] = total[:, f * part : (f + 1) * part]
        for m in range(1, 8):
            fsdp_copy(m).start()
        gain_all[place.f] = gain_parts[place.f]
        while events:
            reduce.step(*events.pop(0)[1:])
        for m in range(1, 8):
            fsdp_copy(m).wait()
        shared = gain_all[0]
        for f in range(1, 8):
            shared += gain_all[f]
        gain_out[...] = shared
        for write in writes:
            write.wait()
        reduce.finish()


def backward(
    queries, keyset, valueset, mixed, grad_mixed, lse, cos_tab, sin_tab, qm, km, gains, second_term,
    normed_one, layer_input, grad_middle, wq_all, narrow_term, wide_term, attn_term,
):
    length, width = queries.shape
    pairs, part = width // PAIR, width // 8
    cuts = [cuts_of(t.shape[1], 3 * PAIR) for t in (narrow_term, wide_term, attn_term)]
    count = pairs + sum(len(c) for c in cuts)
    cols = 3 * PAIR
    block = pl.BlockSpec((length, PAIR), lambda i: (0, i))
    whole = pl.BlockSpec(memory_space=pltpu.VMEM)
    hbm = pl.BlockSpec(memory_space=pl.ANY)
    low = lambda *shape: pltpu.VMEM(shape, jnp.bfloat16)
    wide = lambda *shape: pltpu.VMEM(shape, jnp.float32)
    f32 = lambda *shape: jax.ShapeDtypeStruct(shape, jnp.float32)
    dma = pltpu.SemaphoreType.DMA
    terms = [t.reshape(4, 2, part, t.shape[1]) for t in (narrow_term, wide_term, attn_term)]
    return pl.pallas_call(
        functools.partial(backward_kernel, (pairs, cuts)),
        grid=(pairs,),
        in_specs=[block] * 5
        + [pl.BlockSpec((1, 2, length), lambda i: (i, 0, 0))]
        + [whole] * 7
        + [hbm] * 6,
        out_specs=[hbm] + [whole] * 5,
        out_shape=[
            f32(length, width),
            f32(pairs, part, cols),
            f32(part, attn_term.shape[1]),
            f32(part, wide_term.shape[1]),
            f32(part, narrow_term.shape[1]),
            f32(8, PAIR),
        ],
        scratch_shapes=[
            low(width, length),
            low(length, width),
            wide(length, width),
            low(pairs, 4, 2, part, cols),
            low(pairs, length, cols),
            low(pairs, 4, 2, part, cols),
            low(count, 4, 2, HALF, cols),
            low(count, 4, 2, HALF, cols),
            low(count, 4, 2, STEP, cols),
            low(count, 4, 2 * STEP, cols),
            low(count, 3, 2 * STEP, cols),
            low(count, 2 * STEP, cols),
            low(count, 2 * STEP, cols),
            low(count, HALF, cols),
            low(count, HALF, cols),
            wide(4, 8, width),
            wide(8, 8, PAIR),
            wide(8, 8, PAIR),
            dma((count, 8)),
            dma((count, 8)),
            dma((count,)),
            dma((3,)),
            dma((3,)),
            dma((3,)),
            dma((7,)),
            dma((7,)),
            dma((length // QROWS,)),
        ],
        compiler_params=pltpu.CompilerParams(
            vmem_limit_bytes=62 << 20, collective_id=1, has_side_effects=True
        ),
        cost_estimate=pl.CostEstimate(
            flops=60 * width * length * length, bytes_accessed=40 * length * width,
            transcendentals=pairs * 2 * length * length,
        ),
    )(
        queries, keyset, valueset, mixed, grad_mixed, lse, cos_tab, sin_tab, qm, km, gains, second_term,
        normed_one, layer_input, grad_middle, wq_all, *terms,
    )


def erf_poly(x):
    x = jnp.clip(x, -3.832506856900711, 3.832506856900711)
    sq = x * x
    top = jnp.float32(0.00022905065861350646)
    for coef in (0.0034082910107109506, 0.050955695062380861, 0.18520832239976145, 1.128379143519084):
        top = top * sq + coef
    low = jnp.float32(-1.1791602954361697e-7)
    for coef in (
        0.000023547966471313185, 0.0010179625278914885, 0.014070470171167667, 0.11098505178285362,
        0.49746925110067538, 1.0,
    ):
        low = low * sq + coef
    return x * top / low


def middle_kernel(
    x_ref, mixed_ref, og_ref, km_ref, gain_ref, wa, ww, wn,
    layer_out, go_out, gm_out, second_out, narrow_out, wide_out, attn_out,
    hidden_all, gl_all, gml_all, gt_t, n2_t, mixed_t,
):
    i = pl.program_id(0)
    rows_here, width = x_ref.shape
    half_ff = wn.shape[1]
    tiles = 8
    piece = 3 * PAIR
    rows = pl.ds(pl.multiple_of(i * rows_here, rows_here), rows_here)
    gain = gain_ref[1:2, :]
    mixed = mixed_ref[...]
    middle = x_ref[...].astype(jnp.float32) + jnp.dot(mixed, wa[...], preferred_element_type=jnp.float32)
    c = middle - jnp.mean(middle, axis=1, keepdims=True)
    r2 = lax.rsqrt(jnp.mean(c * c, axis=1, keepdims=True) + eps)
    n2 = c * r2
    low_n2 = (n2 * gain).astype(jnp.bfloat16)
    live = jnp.where(km_ref[:, tiles : tiles + 1].astype(jnp.float32) < -1.0, 0.0, 1.0)
    gt = og_ref[...].astype(jnp.float32) * live
    low_gt = gt.astype(jnp.bfloat16)
    gt_t[:, rows] = jnp.transpose(low_gt)
    n2_t[:, rows] = jnp.transpose(low_n2)
    mixed_t[:, rows] = jnp.transpose(mixed)
    e = jnp.zeros((rows_here, width), jnp.float32)
    out = middle
    for lo in range(0, half_ff, piece):
        at, up = slice(lo, lo + piece), slice(half_ff + lo, half_ff + lo + piece)
        a = jnp.dot(low_n2, ww[:, at], preferred_element_type=jnp.float32)
        gate = jnp.dot(low_n2, ww[:, up], preferred_element_type=jnp.float32)
        gh = jnp.dot(low_gt, wn[:, at], preferred_element_type=jnp.float32)
        cdf = 0.5 + 0.5 * erf_poly(a * (2.0 ** -0.5))
        act = a * cdf
        slope = cdf + a * jnp.exp(a * a * -0.5) * ((2.0 * math.pi) ** -0.5)
        hidden = (act * gate).astype(jnp.bfloat16)
        gl_a = (gh * gate * slope).astype(jnp.bfloat16)
        gl_g = (gh * act).astype(jnp.bfloat16)
        hidden_all[rows, at] = hidden
        gl_all[rows, at] = gl_a
        gl_all[rows, up] = gl_g
        out += rows_dot(hidden, wn[:, at])
        e += rows_dot(gl_a, ww[:, at]) + rows_dot(gl_g, ww[:, up])
    layer_out[...] = out.astype(jnp.bfloat16)
    f2 = e * gain
    gm = gt + r2 * (f2 - jnp.mean(f2, axis=1, keepdims=True) - n2 * jnp.mean(f2 * n2, axis=1, keepdims=True))
    gm_out[...] = gm
    low_gm = gm.astype(jnp.bfloat16)
    gml_all[rows, :] = low_gm
    go_out[...] = rows_dot(low_gm, wa[...]).astype(jnp.bfloat16)
    part = jnp.sum(e * n2, axis=0, keepdims=True)

    @pl.when(i == 0)
    def _():
        second_out[...] = part

    @pl.when(i > 0)
    def _():
        second_out[...] += part

    @pl.when(i == pl.num_programs(0) - 1)
    def _():
        for left, right, term in (
            (gt_t, hidden_all, narrow_out), (n2_t, gl_all, wide_out), (mixed_t, gml_all, attn_out)
        ):
            for lo in range(0, right.shape[1], piece):
                at = slice(lo, lo + piece)
                term[:, at] = jnp.dot(
                    left[...], right[:, at], preferred_element_type=jnp.float32
                ).astype(jnp.bfloat16)


def middle_part(layer_input, mixed, out_grad, km, gains, wa, ww, wn):
    length, width = layer_input.shape
    half_ff = wn.shape[1]
    tile = 2 * TILE
    block = pl.BlockSpec((tile, width), lambda i: (i, 0))
    whole = pl.BlockSpec(memory_space=pltpu.VMEM)
    shape = jax.ShapeDtypeStruct
    low = lambda *dims: pltpu.VMEM(dims, jnp.bfloat16)
    return pl.pallas_call(
        middle_kernel,
        grid=(length // tile,),
        in_specs=[block] * 3 + [pl.BlockSpec((tile, HDIM), lambda i: (i, 0))] + [whole] * 4,
        out_specs=[block] * 3 + [whole] * 4,
        out_shape=[
            shape((length, width), jnp.bfloat16),
            shape((length, width), jnp.bfloat16),
            shape((length, width), jnp.float32),
            shape((1, width), jnp.float32),
            shape((width, half_ff), jnp.bfloat16),
            shape((width, 2 * half_ff), jnp.bfloat16),
            shape((width, width), jnp.bfloat16),
        ],
        scratch_shapes=[
            low(length, half_ff),
            low(length, 2 * half_ff),
            low(length, width),
            low(width, length),
            low(width, length),
            low(width, length),
        ],
        compiler_params=pltpu.CompilerParams(vmem_limit_bytes=60 << 20),
    )(layer_input, mixed, out_grad, km, gains, wa, ww, wn)


def on_device(
    layer_input,
    qkv_weight,
    attn_weight,
    wide_weight,
    narrow_weight,
    first_gain,
    second_gain,
    out_grad,
    token_seg,
    token_live,
):
    gains = jnp.stack([first_gain, second_gain], axis=1)
    gains = jnp.pad(gains, ((0, 0), (0, PAIR - 2)))
    qkv_full, gains = gather_weights([qkv_weight, gains])
    attn_full, wide_full, narrow_full = gather_weights([attn_weight, wide_weight, narrow_weight])
    scale_one = gains[:, 0].astype(jnp.float32)
    scale_two = gains[:, 1].astype(jnp.float32)
    residual_in = layer_input.astype(jnp.float32)
    qm, km = mask_columns(token_seg, token_live)
    cos_tab, sin_tab = rope_tables(token_seg)
    normed_one = layer_norm(residual_in, scale_one).astype(jnp.bfloat16)
    packed = jnp.dot(normed_one, qkv_full, preferred_element_type=jnp.float32)
    queries, keyset, valueset, mixed_rows, lse = attend(packed, cos_tab, sin_tab, qm, km)
    middle = residual_in + jnp.dot(mixed_rows, attn_full, preferred_element_type=jnp.float32)
    normed_two = layer_norm(middle, scale_two).astype(jnp.bfloat16)
    lifted = jnp.dot(normed_two, wide_full, preferred_element_type=jnp.float32)
    hidden = geglu(lifted).astype(jnp.bfloat16)
    layer_out = middle + jnp.einsum(
        "tf,df->td", hidden, narrow_full, preferred_element_type=jnp.float32
    )
    grad_top = out_grad.astype(jnp.float32) * token_live.astype(jnp.float32)[:, None]
    grad_top_low = grad_top.astype(jnp.bfloat16)
    narrow_term = jnp.einsum("td,tf->df", grad_top_low, hidden, preferred_element_type=jnp.float32)
    grad_hidden = jnp.dot(grad_top_low, narrow_full, preferred_element_type=jnp.float32)
    _, pull_gate = jax.vjp(geglu, lifted)
    grad_lifted = pull_gate(grad_hidden)[0].astype(jnp.bfloat16)
    wide_term = jnp.einsum("td,tf->df", normed_two, grad_lifted, preferred_element_type=jnp.float32)
    grad_norm_two = jnp.einsum(
        "tf,df->td", grad_lifted, wide_full, preferred_element_type=jnp.float32
    )
    _, pull_two = jax.vjp(layer_norm, middle, scale_two)
    grad_mid_ln, second_term = pull_two(grad_norm_two)
    grad_middle = grad_top + grad_mid_ln
    grad_middle_low = grad_middle.astype(jnp.bfloat16)
    attn_term = jnp.einsum(
        "td,te->de", mixed_rows, grad_middle_low, preferred_element_type=jnp.float32
    )
    grad_mixed = jnp.einsum(
        "te,de->td", grad_middle_low, attn_full, preferred_element_type=jnp.float32
    )
    shares = scatter_sums([narrow_term, wide_term, attn_term])
    grad_parts = attend_back(
        queries, keyset, valueset, mixed_rows, grad_mixed.astype(jnp.bfloat16), lse,
        cos_tab, sin_tab, qm, km,
    )
    grad_packed = jnp.concatenate(grad_parts, axis=1)
    qkv_term = jnp.einsum("td,tf->df", normed_one, grad_packed, preferred_element_type=jnp.float32)
    grad_norm_one = jnp.einsum(
        "tf,df->td", grad_packed, qkv_full, preferred_element_type=jnp.float32
    )
    _, pull_one = jax.vjp(layer_norm, residual_in, scale_one)
    grad_in_ln, first_term = pull_one(grad_norm_one)
    input_grad = grad_middle + grad_in_ln
    gain_terms = jnp.stack([first_term, second_term], axis=1)
    gain_terms = jnp.pad(gain_terms, ((0, 0), (0, PAIR - 2)))
    qkv_share, gain_share = scatter_sums([qkv_term, gain_terms])
    return (
        layer_out.astype(jnp.bfloat16),
        input_grad,
        qkv_share,
        shares[2],
        shares[1],
        shares[0],
        gain_share[:, 0],
        gain_share[:, 1],
    )


def on_device_tuned(
    layer_input,
    qkv_weight,
    attn_weight,
    wide_weight,
    narrow_weight,
    first_gain,
    second_gain,
    out_grad,
    token_seg,
    token_live,
):
    length, width = layer_input.shape
    pairs, part = width // PAIR, attn_weight.shape[0]
    wq_in = qkv_weight.reshape(part, 3, pairs, PAIR).transpose(2, 0, 1, 3).reshape(pairs, part, 3 * PAIR)
    gain_in = jnp.pad(jnp.stack([first_gain, second_gain]).astype(jnp.float32), ((0, 6), (0, PAIR - part)))
    (queries, keyset, valueset, mixed_rows, lse, normed_one, gains, wq_all, wa_all, ww_all, wn_all,
     cos_tab, sin_tab, qm, km) = forward(
        layer_input, wq_in, attn_weight, wide_weight, narrow_weight, gain_in, token_seg, token_live
    )
    attn_full, wide_full, narrow_full = (w.reshape(width, w.shape[-1]) for w in (wa_all, ww_all, wn_all))
    layer_out, grad_mixed, grad_middle, second_term, *low_terms = middle_part(
        layer_input, mixed_rows, out_grad, km, gains, attn_full, wide_full, narrow_full
    )
    input_grad, qkv_share, attn_share, wide_share, narrow_share, gain_share = backward(
        queries, keyset, valueset, mixed_rows, grad_mixed, lse, cos_tab, sin_tab, qm, km,
        gains, second_term, normed_one, layer_input, grad_middle, wq_all, *low_terms,
    )
    qkv_share = qkv_share.reshape(pairs, part, 3, PAIR).transpose(1, 2, 0, 3).reshape(part, 3 * width)
    return (
        layer_out,
        input_grad,
        qkv_share,
        attn_share,
        wide_share,
        narrow_share,
        gain_share[0, :part],
        gain_share[1, :part],
    )


def solution(mesh):
    tuned = mesh.shape["fsdp"] == 8 and mesh.shape["rep"] == 4
    return jax.shard_map(
        on_device_tuned if tuned else on_device,
        mesh=mesh,
        in_specs=(
            P(("fsdp", "rep"), None),
            P("fsdp", None),
            P("fsdp", None),
            P("fsdp", None),
            P("fsdp", None),
            P("fsdp"),
            P("fsdp"),
            P(("fsdp", "rep"), None),
            P(("fsdp", "rep")),
            P(("fsdp", "rep")),
        ),
        out_specs=(
            P(("fsdp", "rep"), None),
            P(("fsdp", "rep"), None),
            P("fsdp", None),
            P("fsdp", None),
            P("fsdp", None),
            P("fsdp", None),
            P("fsdp"),
            P("fsdp"),
        ),
        check_vma=False,
    )
```

profile of v0, /device:TPU:1, one launch (start us, length us, event | category | flops | bytes accessed | tf_op | source)
XLA Modules:
  0.0 236.8 jit_solution(9436331258014643858)
XLA Ops:
  0.6 1.3 fusion.6.gain_in
  1.9 1.5 reshape.54
  3.4 0.2 copy.22
  3.7 1.1 reshape.55.wq_in
  4.8 71.3 %shard_map.179 = (bf16[1024,768]{1,0:T(8,128)(2,1)}, bf16[1024,768]{1,0:T(8,128)(2,1)}, bf16[1024,768]{1,0:T(8,128)(2,1)}, bf16[1024,768]{1,0:T(8,128)(2,1)}, f3...) custom-call(s32[8,128]{1,0:T(8,128)} %bitcast.26, ...), custom_call_target="tpu_custom_call" | custom-call | flops 17716740096 | bytes 31457280 | tf_op jit(solution)/shard_map/pallas_call | solution.py:649
  76.1 40.1 %shard_map.180 = (bf16[1024,768]{1,0:T(8,128)(2,1)}, bf16[1024,768]{1,0:T(8,128)(2,1)}, f32[1024,768]{1,0:T(8,128)}, f32[1,768]{1,0:T(1,128)}, bf16[768,1152]{1,...) custom-call(bf16[1024,768]{1,0:T(8,128)(2,1)} %x_in.1, ...), custom_call_target="tpu_custom_call" | custom-call | tf_op jit(solution)/shard_map/pallas_call | solution.py:1229
  116.2 109.7 %shard_map.181 = (f32[1024,768]{1,0:T(8,128)}, f32[6,96,384]{2,1,0:T(8,128)}, f32[96,768]{1,0:T(8,128)}, f32[96,2304]{1,0:T(8,128)}, f32[96,1152]{1,0:T(8,128)}, /*index=5*/f32[8,128]{1,0:T(8,128)}) custom-call(bf16[1024,768]{1,0:T(8,128)(2,1)} %get-tuple-element.43.q_ref, bf16[1024,768]{1,0:T(8,128)(2,1)} %get-tuple-element.44.k_ref, ...), custom_call_target="tpu_custom_call" | custom-call | flops 48318382080 | bytes 31457280 | tf_op jit(solution)/shard_map/pallas_call | solution.py:1077
  225.9 1.3 slice_bitcast_fusion
  227.2 1.5 reshape.62
  228.7 0.5 copy.23
  229.2 1.1 reshape.63
  230.3 0.0 copy-start.2
  230.3 0.0 copy-start
  230.3 3.9 %copy.28 = f32[1024,768]{1,0:T(8,128)} copy(f32[1024,768]{1,0:T(8,128)} %get-tuple-element.75) | data formatting | bytes 6291456
  234.2 0.0 copy-done.2
  234.2 0.0 copy-start.1
  234.2 0.7 copy.29
  234.9 0.0 copy-done
  234.9 0.9 copy.30
  235.8 0.0 copy-done.1
  235.8 0.8 copy.31
Async XLA Ops:
  230.3 3.9 %copy-start.2 = (f32[96,768]{1,0:T(8,128)S(1)}, f32[96,768]{1,0:T(8,128)}, u32[]{:S(2)}) copy-start(f32[96,768]{1,0:T(8,128)} %get-tuple-element.77) | copy-start | bytes 884740
  230.3 4.6 %copy-start = (f32[96,2304]{1,0:T(8,128)S(1)}, f32[96,2304]{1,0:T(8,128)}, u32[]{:S(2)}) copy-start(f32[96,2304]{1,0:T(8,128)} %get-tuple-element.78) | copy-start | bytes 2654212
  234.2 1.6 copy-start.1
where the time goes:
time: 237 us
  Pallas kernels  221 us (93%)
  local copies, waits for them, and re-layouts  13.5 us (6%)
    pallas_call x1, Pallas kernels, backward(): pl.pallas_call(functools.partial(backward_kernel, (pairs, cuts)), grid=(p...  110 us
    pallas_call x1, Pallas kernels, forward(): pl.pallas_call(functools.partial(forward_kernel, (pairs, cuts)), grid=(pa...  71.3 us
    pallas_call x1, Pallas kernels, middle_part(): pl.pallas_call(middle_kernel, grid=(length // tile,), in_specs=[block] *...  40.1 us
    unnamed x10, local copies, waits for them, and re-layouts  6.25 us

commit v1 on v0

--- a/solution.py
+++ b/solution.py
@@ -277,6 +277,7 @@
 MESH = pl.DeviceIdType.MESH
 HALF = 48
 AHEAD = 4
+FORWARD_CUT = 768
 GATHER_LAGS = (3.0 - 2.1 * AHEAD, 3.0, 7.5, 12.0, 15.0)
 PACE = 2.1
 PAIR_US = 6.0
@@ -349,8 +350,12 @@
     )
 
 
-def staged(count, lags, pace):
-    return sorted((lag + pace * k, stage, k) for stage, lag in enumerate(lags) for k in range(count))
+def staged(units, lags, pace):
+    return sorted(
+        (lag + pace * (sum(units[:k]) + stage * (unit - 1)), stage, k)
+        for stage, lag in enumerate(lags)
+        for k, unit in enumerate(units)
+    )
 
 
 class Gather:
@@ -477,7 +482,8 @@
             targets.append(full.at[:, :, :, pl.ds(lo, size)])
     gather = Gather(place, sources, targets, send, recv, own)
 
-    events = staged(gather.count, GATHER_LAGS, PACE)
+    units = [1] * npairs + [size / (3 * PAIR) for cut in cuts for _, size in cut]
+    events = staged(units, GATHER_LAGS, PACE)
     events = [e for e in events if e[1:] not in [(0, k) for k in range(AHEAD)]]
 
     def run_until(time):
@@ -551,15 +557,14 @@
         gain_out[...] = gains
         run_until(6.4)
 
-        def norm_rows(b, carry):
-            rows = pl.ds(pl.multiple_of(b * TILE, TILE), TILE)
+        for b in range(tiles):
+            rows = slice(b * TILE, (b + 1) * TILE)
             v = x_ref[rows, :].astype(jnp.float32)
             c = v - jnp.mean(v, axis=1, keepdims=True)
             spread = jnp.mean(c * c, axis=1, keepdims=True)
             normed_out[rows, :] = (c * lax.rsqrt(spread + eps) * gain_out[0:1, :]).astype(jnp.bfloat16)
-            return carry
-
-        lax.fori_loop(0, tiles, norm_rows, 0)
+            if b % 2:
+                run_until(6.4 + b)
         run_until(GATHER_LAGS[4])
         load(0).start()
         load(0).wait()
@@ -639,7 +644,7 @@
     pairs = width // PAIR
     part = attn_weight.shape[0]
     cos_c, sin_c = table_constants(length)
-    cuts = [cuts_of(w.shape[1], 3 * PAIR) for w in (attn_weight, wide_weight, narrow_weight)]
+    cuts = [cuts_of(w.shape[1], FORWARD_CUT) for w in (attn_weight, wide_weight, narrow_weight)]
     count = pairs + sum(len(c) for c in cuts)
     block = pl.BlockSpec((length, PAIR), lambda i: (0, i))
     whole = pl.BlockSpec(memory_space=pltpu.VMEM)
@@ -756,6 +761,12 @@
             self.f.at[k], self.rf.at[k], self.send.at[k, 7], self.recv.at[k, 7], self.p.core_dev()
         )
 
+    def put(self, k, rows, sums):
+        ref, starts = self.outs[k]
+        size = sums.shape[1] // len(starts)
+        for j, lo in enumerate(starts):
+            ref[rows, lo : lo + size] = sums[:, j * size : (j + 1) * size].astype(jnp.float32)
+
     def plus(self, a, b):
         return (a.astype(jnp.float32) + b.astype(jnp.float32)).astype(jnp.bfloat16)
 
@@ -799,10 +810,10 @@
             self.f[k, STEP : 2 * STEP, :] = self.plus(self.s[k, high, :], self.ry2[k, low, :])
             self.f[k, self.local(2 * STEP * (1 - p.y), STEP), :] = self.ry2[k, high, :]
             self.core2_copy(k).start()
-            self.outs[k][p.rows_core(), :] = self.f[k].astype(jnp.float32)
+            self.put(k, p.rows_core(), self.f[k])
         else:
             self.core2_copy(k).wait_recv()
-            self.outs[k][self.local(HALF * (1 - p.core), HALF), :] = self.rf[k].astype(jnp.float32)
+            self.put(k, self.local(HALF * (1 - p.core), HALF), self.rf[k])
 
     def finish(self):
         for k in range(self.count):
@@ -817,6 +828,7 @@
 
 REDUCE_LAGS = (0.0, 4.0, 10.0, 16.0, 22.0, 28.0, 32.0)
 BACK_US = 8.6
+SPACING = 4
 
 
 def reduce_events(given, pairs):
@@ -899,12 +911,12 @@
     for cut, term, out in zip(cuts, (narrow_in, wide_in, attn_in), (narrow_out, wide_out, attn_out)):
         for lo, size in cut:
             sources.append(term.at[:, :, :, pl.ds(lo, size)])
-            outs.append(out.at[:, pl.ds(lo, size)])
+            outs.append((out, [lo]))
             loaded.append(True)
     given = len(sources)
     for p in range(npairs):
         sources.append(terms.at[p])
-        outs.append(qkv_out.at[p])
+        outs.append((qkv_out, [j * width + p * PAIR for j in range(3)]))
         loaded.append(False)
     bufs = (acc, rc, ry, rx, rz, s_buf, ry2, f_buf, rf)
     reduce = Reduce(place, sources, loaded, outs, bufs, send, recv, load)
@@ -914,6 +926,8 @@
     for p in range(npairs):
         for slot in range(slots + 1):
             now = BACK_US * (p + min(slot, slots - 0.01) / slots) if slot < slots else BACK_US * (p + 1)
+            if slot % SPACING:
+                continue
             while events and events[0][0] <= now:
                 queue[p][slot].append(events.pop(0)[1:])
 
@@ -956,7 +970,8 @@
         grad_v = jnp.zeros((length, HDIM), jnp.float32)
         grad_q = []
         for begin in range(0, length, QROWS):
-            run_slot(slot)
+            if slot % SPACING == 0:
+                run_slot(slot)
             slot += 1
             span = slice(begin, begin + QROWS)
             low_q, low_go = q_ref[span, cols], go_ref[span, cols]
@@ -1084,7 +1099,7 @@
         out_specs=[hbm] + [whole] * 5,
         out_shape=[
             f32(length, width),
-            f32(pairs, part, cols),
+            f32(part, 3 * width),
             f32(part, attn_term.shape[1]),
             f32(part, wide_term.shape[1]),
             f32(part, narrow_term.shape[1]),
@@ -1359,7 +1374,6 @@
         queries, keyset, valueset, mixed_rows, grad_mixed, lse, cos_tab, sin_tab, qm, km,
         gains, second_term, normed_one, layer_input, grad_middle, wq_all, *low_terms,
     )
-    qkv_share = qkv_share.reshape(pairs, part, 3, PAIR).transpose(1, 2, 0, 3).reshape(part, 3 * width)
     return (
         layer_out,
         input_grad,

time: 237 us -> 230 us (0.970)
  Pallas kernels: 221 us -> 215 us
    pallas_call x1, Pallas kernels: 110 us -> 104 us  [backward(): pl.pallas_call(functools.partial(backward_kernel, (pairs, cuts)), grid=(p...]
    reshape x2 -> x0, local copies, waits for them, and re-layouts: 2.58 us -> none  [on_device_tuned(): qkv_share.reshape(pairs, part, 3, PAIR).transpose(1, 2, 0, 3)]
    unnamed x10 -> x13, local copies, waits for them, and re-layouts: 6.25 us -> 7.36 us
where the time goes in v1:
time: 230 us; the launch traced here: 229 us
  Pallas kernels  215 us (93%)
  local copies, waits for them, and re-layouts  11.5 us (5%)
    pallas_call x1, Pallas kernels, backward(): pl.pallas_call(functools.partial(backward_kernel, (pairs, cuts)), grid=(p...  104 us
    pallas_call x1, Pallas kernels, forward(): pl.pallas_call(functools.partial(forward_kernel, (pairs, cuts)), grid=(pa...  70.7 us
    pallas_call x1, Pallas kernels, middle_part(): pl.pallas_call(middle_kernel, grid=(length // tile,), in_specs=[block] *...  40.1 us
    unnamed x13, local copies, waits for them, and re-layouts  7.36 us

profile of v1, /device:TPU:1, one launch (start us, length us, event | category | flops | bytes accessed | tf_op | source)
XLA Modules:
  0.0 228.7 jit_solution(8280787245264706521)
XLA Ops:
  0.6 1.3 fusion.6.gain_in
  1.9 1.5 reshape.48
  3.4 0.2 copy.21
  3.7 1.1 reshape.49.wq_in
  4.8 70.7 %shard_map.179 = (bf16[1024,768]{1,0:T(8,128)(2,1)}, bf16[1024,768]{1,0:T(8,128)(2,1)}, bf16[1024,768]{1,0:T(8,128)(2,1)}, bf16[1024,768]{1,0:T(8,128)(2,1)}, f3...) custom-call(s32[8,128]{1,0:T(8,128)} %bitcast.24, ...), custom_call_target="tpu_custom_call" | custom-call | flops 17716740096 | bytes 31457280 | tf_op jit(solution)/shard_map/pallas_call | solution.py:654
  75.6 40.1 %shard_map.180 = (bf16[1024,768]{1,0:T(8,128)(2,1)}, bf16[1024,768]{1,0:T(8,128)(2,1)}, f32[1024,768]{1,0:T(8,128)}, f32[1,768]{1,0:T(1,128)}, bf16[768,1152]{1,...) custom-call(bf16[1024,768]{1,0:T(8,128)(2,1)} %x_in.1, ...), custom_call_target="tpu_custom_call" | custom-call | tf_op jit(solution)/shard_map/pallas_call | solution.py:1244
  115.7 104.2 %shard_map.181 = (f32[1024,768]{1,0:T(8,128)}, f32[96,2304]{1,0:T(8,128)}, f32[96,768]{1,0:T(8,128)}, f32[96,2304]{1,0:T(8,128)}, f32[96,1152]{1,0:T(8,128)}, /*index=5*/f32[8,128]{1,0:T(8,128)}) custom-call(bf16[1024,768]{1,0:T(8,128)(2,1)} %get-tuple-element.43.q_ref, bf16[1024,768]{1,0:T(8,128)(2,1)} %get-tuple-element.44.k_ref, ...), custom_call_target="tpu_custom_call" | custom-call | flops 48318382080 | bytes 31457280 | tf_op jit(solution)/shard_map/pallas_call | solution.py:1092
  219.9 1.3 slice_bitcast_fusion
  221.1 0.0 copy-start.1
  221.1 3.8 %copy.27 = f32[1024,768]{1,0:T(8,128)} copy(f32[1024,768]{1,0:T(8,128)} %get-tuple-element.75) | data formatting | bytes 6291456
  225.0 0.0 copy-done.1
  225.0 0.0 copy-start.3
  225.0 0.0 copy-start
  225.0 0.9 copy.28
  225.9 0.2 copy-done.3
  226.1 0.0 copy-start.2
  226.1 0.7 copy.29
  226.8 0.0 copy-done
  226.8 0.9 copy.30
  227.7 0.0 copy-done.2
  227.7 0.8 copy.31
Async XLA Ops:
  221.1 3.8 %copy-start.1 = (f32[96,2304]{1,0:T(8,128)S(1)}, f32[96,2304]{1,0:T(8,128)}, u32[]{:S(2)}) copy-start(f32[96,2304]{1,0:T(8,128)} %get-tuple-element.76) | copy-start | bytes 2654212
  225.0 1.1 copy-start.3
  225.0 1.8 copy-start
  226.1 1.6 copy-start.2
